TPU v7x, 32 devices: a whole 2x2x4 slice. The times are simulated.
32 devices in a mesh: ctx: 8 (over y, x, core), exp: 4 (over z).
Axes of the slice: x: 2, y: 2, z: 4, core: 2. Of those that a mesh axis runs over, the one named last changes fastest.
Arguments:
- inputs: bfloat16 [1024, 1024], P('exp', 'ctx'), may hold values from -6 to 6
- conv_taps: float32 [1024, 31], P('exp'), may hold values from -1 to 1
- norm_gain: bfloat16 [1024], P('exp'), may hold values from 0.099609375 to 1.8984375
- routes: int32 [1024, 2], P('ctx'), may hold values from 0 to 7, all different within a row; in each aligned block of 128 rows (0 to 127, 128 to 255, ...) at most 32 rows name the same one
- gate_probs: float32 [1024, 2], P('ctx'), may hold values from 0.1 to 0.9
- w_gate: bfloat16 [8, 1024, 4096], P('ctx', None, 'exp'), may hold values from -0.1875 to 0.1875
- w_up: bfloat16 [8, 1024, 4096], P('ctx', None, 'exp'), may hold values from -0.1875 to 0.1875
- w_down: bfloat16 [8, 4096, 1024], P('ctx', 'exp'), may hold values from -0.09375 to 0.09375
- grad_out: bfloat16 [1024, 1024], P('exp', 'ctx'), may hold values from -6 to 6
Outputs:
- layer_out: bfloat16 [1024, 1024], P('exp', 'ctx')
- grad_inputs: bfloat16 [1024, 1024], P('exp', 'ctx')
- grad_taps: float32 [1024, 31], P('exp')
- grad_gain: float32 [1024], P('exp')
- grad_gates: float32 [1024, 2], P('ctx')
- grad_w_gate: bfloat16 [8, 1024, 4096], P('ctx', None, 'exp')
- grad_w_up: bfloat16 [8, 1024, 4096], P('ctx', None, 'exp')
- grad_w_down: bfloat16 [8, 4096, 1024], P('ctx', 'exp')
Inputs may be any that keep to these rules, and one draw needn't show every extreme that they name: `routes`: in each aligned block of 128 rows (the rows of one index of ctx) no expert is named by more than 32 rows, a bound that some block reaches; the two experts of a row differ.
All inputs are finite; a program needn't handle non-finite values.
Results may differ from a plain program's by a relative error of at most 0.025.
Values may be sent and summed in bfloat16 or wider, within the bound.
A program may use at most 64 MiB of HBM per device.

v0:
```python
import jax
import jax.numpy as jnp
from jax import lax
from jax.sharding import PartitionSpec as P

EPS = 1e-05


def padded_2(cells, sides, width):
    for axis, dim in sides:
        count = lax.axis_size(axis)
        head = lax.slice_in_dim(cells, 0, width, axis=dim)
        tail = lax.slice_in_dim(cells, cells.shape[dim] - width, cells.shape[dim], axis=dim)
        cells = jnp.concatenate(
            [
                lax.ppermute(tail, axis, [(i, (i + 1) % count) for i in range(count)]),
                cells,
                lax.ppermute(head, axis, [((i + 1) % count, i) for i in range(count)]),
            ],
            axis=dim,
        )
    return cells


def shortened(x):

    def short(part):
        return part.astype(jnp.bfloat16) if part.dtype == jnp.float32 else part

    return jax.tree.map(short, x)


def slot_rows(routes, experts, capacity):
    flat = routes.reshape(-1)
    onehot = (flat[:, None] == jnp.arange(experts, dtype=jnp.int32)[None, :]).astype(jnp.int32)
    before = jnp.cumsum(onehot, axis=0, dtype=jnp.int32) - onehot
    place = jnp.sum(before * onehot, axis=1, dtype=jnp.int32)
    return flat * capacity + place


def bring_back(values, dest, weights, experts, capacity, whole_cot):
    width = values.shape[1]
    back = lax.all_to_all(
        values.reshape(experts, capacity, width).astype(jnp.bfloat16),
        "ctx",
        split_axis=0,
        concat_axis=0,
        tiled=True,
    ).astype(jnp.float32)
    picked = back.reshape(experts * capacity, width)[dest]
    term = jnp.sum((picked * weights[:, None]).reshape(-1, 2, width), axis=1)
    share = lax.psum_scatter(
        term.astype(jnp.bfloat16), "exp", scatter_dimension=1, tiled=True
    ).astype(jnp.float32)
    dots = None if whole_cot is None else jnp.sum(picked * whole_cot, axis=1)
    return (share, dots)


def local(inputs, conv_taps, norm_gain, routes, gate_probs, w_gate, w_up, w_down, grad_out):
    chans, tokens = inputs.shape
    taps = conv_taps.shape[1]
    half = taps // 2
    width = w_gate.shape[1]
    experts = lax.axis_size("ctx")
    capacity = max(tokens // 8, (2 * tokens + experts - 1) // experts)
    padded = padded_2(inputs, (("ctx", 1),), half)
    padded_f = padded.astype(jnp.float32)
    conv = jnp.zeros((chans, tokens), jnp.float32)
    for offset in range(taps):
        conv = conv + conv_taps[:, offset : offset + 1] * padded_f[:, offset : offset + tokens]
    mixed = (inputs.astype(jnp.float32) + conv).astype(jnp.bfloat16)
    mixed_f = mixed.astype(jnp.float32)
    gain_f = norm_gain.astype(jnp.float32)
    squares = lax.psum(jnp.sum(mixed_f * mixed_f, axis=0), "exp")
    scale = lax.rsqrt(squares / width + EPS)
    normed_part = (mixed_f * gain_f[:, None] * scale[None, :]).astype(jnp.bfloat16)
    normed, cotangent = (
        lax.all_gather(normed_part, "exp", axis=0, tiled=True),
        lax.all_gather(grad_out, "exp", axis=0, tiled=True),
    )
    dest = slot_rows(routes, experts, capacity)
    gates = gate_probs.reshape(-1)
    cot_rows = jnp.repeat(cotangent.T, 2, axis=0).astype(jnp.float32)
    token_rows = jnp.repeat(normed.T, 2, axis=0)
    scaled_rows = (cot_rows * gates[:, None]).astype(jnp.bfloat16)
    empty = jnp.zeros((experts * capacity, width), jnp.bfloat16)
    send_x = empty.at[dest].set(token_rows).reshape(experts, capacity, width)
    send_dy = empty.at[dest].set(scaled_rows).reshape(experts, capacity, width)
    recv_x, recv_dy = (
        lax.all_to_all(send_x, "ctx", split_axis=0, concat_axis=0, tiled=True),
        lax.all_to_all(send_dy, "ctx", split_axis=0, concat_axis=0, tiled=True),
    )
    rows_x = recv_x.reshape(-1, width)
    rows_dy = recv_dy.reshape(-1, width)
    weight_gate = w_gate[0]
    weight_up = w_up[0]
    weight_down = w_down[0]
    gate_act = jnp.dot(rows_x, weight_gate, preferred_element_type=jnp.float32)
    up_act = jnp.dot(rows_x, weight_up, preferred_element_type=jnp.float32)
    sigma = jax.nn.sigmoid(gate_act)
    hidden = (gate_act * sigma * up_act).astype(jnp.bfloat16)
    partial_out = jnp.dot(hidden, weight_down, preferred_element_type=jnp.float32)
    moe_share, gate_dots = bring_back(partial_out, dest, gates, experts, capacity, cot_rows)
    layer_out = (mixed_f + moe_share.T).astype(jnp.bfloat16)
    grad_gates = lax.psum(gate_dots, "exp").reshape(tokens, 2)
    contract_last = (((1,), (1,)), ((), ()))
    contract_first = (((0,), (0,)), ((), ()))
    d_hidden = lax.dot_general(
        rows_dy, weight_down, contract_last, preferred_element_type=jnp.float32
    )
    grad_down = lax.dot_general(
        hidden, rows_dy, contract_first, preferred_element_type=jnp.float32
    ).astype(jnp.bfloat16)
    d_gate = (d_hidden * up_act * sigma * (1.0 + gate_act * (1.0 - sigma))).astype(jnp.bfloat16)
    d_up = (d_hidden * gate_act * sigma).astype(jnp.bfloat16)
    grad_gate = lax.dot_general(
        rows_x, d_gate, contract_first, preferred_element_type=jnp.float32
    ).astype(jnp.bfloat16)
    grad_up = lax.dot_general(
        rows_x, d_up, contract_first, preferred_element_type=jnp.float32
    ).astype(jnp.bfloat16)
    d_rows = lax.dot_general(d_gate, weight_gate, contract_last, preferred_element_type=jnp.float32)
    d_rows = d_rows + lax.dot_general(
        d_up, weight_up, contract_last, preferred_element_type=jnp.float32
    )
    d_share, unused_dots = bring_back(d_rows, dest, jnp.ones_like(gates), experts, capacity, None)
    d_normed = d_share.T
    gain_local = jnp.sum(d_normed * mixed_f * scale[None, :], axis=1)
    norm_terms = lax.psum(jnp.sum(d_normed * gain_f[:, None] * mixed_f, axis=0), "exp")
    cot_own = grad_out.astype(jnp.float32)
    d_mixed = (
        cot_own
        + gain_f[:, None] * d_normed * scale[None, :]
        - mixed_f * (norm_terms * scale * scale * scale / width)[None, :]
    )
    grad_padded = padded_2(shortened(d_mixed), (("ctx", 1),), half).astype(d_mixed.dtype)
    grad_in = d_mixed
    tap_parts = []
    for offset in range(taps):
        grad_in = (
            grad_in
            + conv_taps[:, offset : offset + 1]
            * grad_padded[:, 2 * half - offset : 2 * half - offset + tokens]
        )
        tap_parts.append(jnp.sum(d_mixed * padded_f[:, offset : offset + tokens], axis=1))
    tap_local = jnp.stack(tap_parts, axis=1)
    grad_taps, grad_gain = lax.psum((tap_local, gain_local), "ctx")
    return (
        layer_out,
        grad_in.astype(jnp.bfloat16),
        grad_taps,
        grad_gain,
        grad_gates,
        grad_gate[None],
        grad_up[None],
        grad_down[None],
    )


def solution(mesh):
    return jax.shard_map(
        local,
        mesh=mesh,
        in_specs=(
            P("exp", "ctx"),
            P("exp", None),
            P("exp"),
            P("ctx", None),
            P("ctx", None),
            P("ctx", None, "exp"),
            P("ctx", None, "exp"),
            P("ctx", "exp", None),
            P("exp", "ctx"),
        ),
        out_specs=(
            P("exp", "ctx"),
            P("exp", "ctx"),
            P("exp", None),
            P("exp"),
            P("ctx", None),
            P("ctx", None, "exp"),
            P("ctx", None, "exp"),
            P("ctx", "exp", None),
        ),
        check_vma=False,
    )
```

profile of v0, /device:TPU:1, one launch (start us, length us, event | category | flops | bytes accessed | tf_op | source)
XLA Modules:
  0.0 211.1 jit_solution(18306011151170475799)
XLA Ops:
  8.3 2.7 %collective-permute-start = (bf16[256,15]{0,1:T(8,128)(2,1)S(1)}, bf16[256,15]{0,1:T(8,128)(2,1)S(1)}, u32[]{:S(2)}, u32[]{:S(2)}) collective-permute-start(bf16[256,15]{0,1:T(8,128)(2,1)S(1)} %get-tuple-element.71), channel_id=1, source_target_pairs={{0,4},{4,8},{8,12},{12,16},{16,20},{20,24},{24,28},{28,0},{1,5},{5... | collective-permute-start | bytes 23048 | tf_op jit(solution)/shard_map/ppermute | solution.py:16
  14.7 11.5 %all_gather.7 = bf16[1024,128]{1,0:T(8,128)(2,1)S(1)} all-gather(bf16[256,128]{1,0:T(8,128)(2,1)} %param.17), channel_id=1, replica_groups=mesh['ctx'=8,'exp'=4] {'exp'}, dimensions={0}, use_global_device_ids=true | all-gather | bytes 327680 | tf_op jit(solution)/shard_map/all_gather | solution.py:79
  27.8 1.9 convert_element_type.108
  29.9 2.5 %scatter_custom_fusion.1 = bf16[256,1024]{1,0:T(8,128)(2,1)} fusion(s32[256]{0:T(256)S(1)} %bitcast.245, f32[256,1024]{1,0:T(8,128)S(1)} %convert_element_type.108, f32[256]{0:T(256)S(1)} %mul.828, bf16[]{:T(256)} %constant.8.clone.1), kind=kCustom, calls=%fused_computation.29 | custom fusion | flops 524288 | bytes 1573890 | tf_op jit(solution)/shard_map/scatter | solution.py:88
  32.4 8.4 %all-to-all-start.2 = ((bf16[8,32,1024]{2,1,0:T(8,128)(2,1)}), bf16[8,32,1024]{2,1,0:T(8,128)(2,1)}, u32[]{:S(2)}, u32[]{:S(2)}) async-start(bf16[8,32,1024]{2,1,0:T(8,128)(2,1)} %bitcast.149), calls=%async_computation.3 | async-start | bytes 1048576 | tf_op jit(solution)/shard_map/all_to_all | solution.py:91
  42.3 9.9 %psum.35 = f32[128]{0:T(128)S(1)} all-reduce(f32[128]{0:T(128)} %get-tuple-element.62), channel_id=1, replica_groups=mesh['ctx'=8,'exp'=4] {'exp'}, use_global_device_ids=true, to_apply=%region_4.5 | all-reduce | flops 128 | bytes 1024 | tf_op jit(solution)/shard_map/psum | solution.py:74
  52.7 11.0 %all_gather.6 = bf16[1024,128]{0,1:T(8,128)(2,1)S(1)} all-gather(bf16[256,128]{0,1:T(8,128)(2,1)S(1)} %fusion.27), channel_id=1, replica_groups=mesh['ctx'=8,'exp'=4] {'exp'}, dimensions={0}, use_global_device_ids=true | all-gather | bytes 327680 | tf_op jit(solution)/shard_map/all_gather | solution.py:78
  64.2 2.6 %scatter_custom_fusion = bf16[256,1024]{1,0:T(8,128)(2,1)} fusion(s32[256]{0:T(256)} %bitcast.246, bf16[256,1024]{1,0:T(8,128)(2,1)S(1)} %reshape.158, bf16[]{:T(256)} %constant.8.clone.1), kind=kCustom, calls=%fused_computation.41 | custom fusion | bytes 524800 | tf_op jit(solution)/shard_map/scatter | solution.py:87
  66.8 9.1 %all-to-all-start = ((bf16[8,32,1024]{2,1,0:T(8,128)(2,1)}), bf16[8,32,1024]{2,1,0:T(8,128)(2,1)S(1)}, u32[]{:S(2)}, u32[]{:S(2)}) async-start(bf16[8,32,1024]{2,1,0:T(8,128)(2,1)} %bitcast.36), calls=%async_computation | async-start | bytes 1048576 | tf_op jit(solution)/shard_map/all_to_all | solution.py:90
  76.6 3.5 %fusion.2 = f32[256,1024]{1,0:T(8,128)} fusion(bf16[256,1024]{1,0:T(8,128)(2,1)} %bitcast.47, bf16[1,1024,1024]{2,1,0:T(8,128)(2,1)} %param.16), kind=kOutput, calls=%fused_computation.6 | convolution fusion | flops 536870912 | bytes 3670016 | tf_op jit(solution)/shard_map/dot_general | solution.py:108
  80.1 2.6 %all-to-all-done = bf16[8,32,1024]{2,1,0:T(8,128)(2,1)S(1)} async-done(((bf16[8,32,1024]{2,1,0:T(8,128)(2,1)}), bf16[8,32,1024]{2,1,0:T(8,128)(2,1)S(1)}, u32[]{:S(2)}, u32[]{:S(2)}) %all-to-all-start) | async-done | bytes 524320 | tf_op jit(solution)/shard_map/all_to_all | solution.py:90
  82.6 2.5 %fusion.6 = f32[256,1024]{1,0:T(8,128)S(1)} fusion(bf16[256,1024]{1,0:T(8,128)(2,1)S(1)} %bitcast.145, bf16[1,1024,1024]{2,1,0:T(8,128)(2,1)} %param.15), kind=kOutput, calls=%fused_computation.10 | convolution fusion | flops 536870912 | bytes 3670016 | tf_op jit(solution)/shard_map/dot_general | solution.py:99
  85.2 2.0 multiply_convert_fusion.1
  88.0 1.5 fusion.15
  89.5 6.4 %all-to-all-start.1 = ((bf16[8,32,1024]{2,1,0:T(8,128)(2,1)}), bf16[8,32,1024]{2,1,0:T(8,128)(2,1)S(1)}, u32[]{:S(2)}, u32[]{:S(2)}) async-start(bf16[8,32,1024]{2,1,0:T(8,128)(2,1)} %fusion.15), calls=%async_computation.1 | async-start | bytes 1048576 | tf_op jit(solution)/shard_map/all_to_all | solution.py:43
  95.9 2.4 %fusion.4 = f32[256,1024]{1,0:T(8,128)S(1)} fusion(bf16[256,1024]{1,0:T(8,128)(2,1)S(1)} %get-tuple-element.66, bf16[1,1024,1024]{2,1,0:T(8,128)(2,1)} %param.15), kind=kOutput, calls=%fused_computation.8 | convolution fusion | flops 536870912 | bytes 3670016 | tf_op jit(solution)/shard_map/dot_general | solution.py:123
  98.3 1.6 fusion.18
  99.9 2.8 %all-to-all-done.1 = bf16[8,32,1024]{2,1,0:T(8,128)(2,1)S(1)} async-done(((bf16[8,32,1024]{2,1,0:T(8,128)(2,1)}), bf16[8,32,1024]{2,1,0:T(8,128)(2,1)S(1)}, u32[]{:S(2)}, u32[]{:S(2)}) %all-to-all-start.1) | async-done | bytes 524320 | tf_op jit(solution)/shard_map/all_to_all | solution.py:43
  102.7 7.1 %all-to-all-start.3 = ((bf16[8,32,1024]{2,1,0:T(8,128)(2,1)}), bf16[8,32,1024]{2,1,0:T(8,128)(2,1)}, u32[]{:S(2)}, u32[]{:S(2)}) async-start(bf16[8,32,1024]{2,1,0:T(8,128)(2,1)} %bitcast.48), calls=%async_computation.4 | async-start | bytes 1048576 | tf_op jit(solution)/shard_map/all_to_all | solution.py:43
  110.9 2.1 gather_fusion
  113.0 2.9 %gather.9 = f32[128,2,1024]{2,1,0:T(2,128)} reshape(f32[256,1024]{1,0:T(8,128)} %gather_fusion) | data formatting | bytes 2097152 | tf_op jit(solution)/shard_map/gather | solution.py:50
  115.9 3.3 %multiply_reduce_fusion.1 = bf16[128,1024]{1,0:T(8,128)(2,1)} fusion(f32[128,2,1024]{2,1,0:T(2,128)} %gather.9, f32[128,2]{1,0:T(8,128)S(1)} %copy.35), kind=kLoop, calls=%fused_computation.26 | loop fusion | flops 393216 | bytes 1311744 | tf_op jit(solution)/shard_map/reduce_sum | solution.py:51
  119.5 2.1 convert_bitcast_fusion.2
  122.7 2.0 gather_fusion.1
  124.7 2.9 %reshape.132 = f32[128,2,1024]{2,1,0:T(2,128)} reshape(f32[256,1024]{1,0:T(8,128)} %gather_fusion.1) | data formatting | bytes 2097152 | tf_op jit(solution)/shard_map/reshape | solution.py:51
  127.6 3.2 %reduce_sum.348 = bf16[128,1024]{1,0:T(8,128)(2,1)} reduce(f32[128,2,1024]{2,1,0:T(2,128)} %reshape.132, f32[]{:T(128)} %constant.7.clone.1), dimensions={1}, to_apply=%region_9.10 | reduce | flops 131072 | bytes 1310724 | tf_op jit(solution)/shard_map/reduce_sum | solution.py:51
  130.9 2.1 convert_bitcast_fusion.1
  132.9 3.3 %convert_bitcast_fusion = bf16[1,1024,1024]{2,1,0:T(8,128)(2,1)} fusion(bf16[256,1024]{1,0:T(8,128)(2,1)S(1)} %copy-done.15, bf16[256,1024]{1,0:T(8,128)(2,1)} %bitcast.47), kind=kOutput, calls=%fused_computation.16 | convolution fusion | flops 537919488 | bytes 3145728 | tf_op jit(solution)/shard_map/dot_general | solution.py:111
  136.6 19.3 %reduce-scatter.5.cloned.1.call-done = bf16[128,256]{1,0:T(8,128)(2,1)} async-done(((bf16[128,1024]{1,0:T(8,128)(2,1)}), bf16[128,256]{1,0:T(8,128)(2,1)}) %reduce-scatter.5.cloned.1.call-update) | async-done | bytes 65552 | tf_op jit(solution)/shard_map/reduce_scatter | solution.py:52
  156.9 13.4 %all-reduce.1 = (f32[128]{0:T(128)S(1)}, f32[128,2]{1,0:T(8,128)S(1)}) all-reduce(f32[128]{0:T(128)S(1)} %get-tuple-element.56, f32[128,2]{1,0:T(8,128)S(1)} %reshape.133), channel_id=1, replica_groups=mesh['ctx'=8,'exp'=4] {'exp'}, use_global_device_ids=true, to_apply=%region_12.13 | all-reduce | flops 384 | bytes 3072 | tf_op jit(solution)/shard_map/psum | solution.py:129
  172.0 7.2 %collective-permute-start.2 = (bf16[256,15]{0,1:T(8,128)(2,1)S(1)}, bf16[256,15]{0,1:T(8,128)(2,1)S(1)}, u32[]{:S(2)}, u32[]{:S(2)}) collective-permute-start(bf16[256,15]{0,1:T(8,128)(2,1)S(1)} %get-tuple-element.68), channel_id=1, source_target_pairs={{0,4},{4,8},{8,12},{12,16},{16,20},{20,24},{24,28},{28,0},{1,5},{5... | collective-permute-start | bytes 23048 | tf_op jit(solution)/shard_map/ppermute | solution.py:16
  179.3 22.2 %all-reduce = (f32[256,31]{0,1:T(8,128)}, f32[256]{0:T(256)}) all-reduce(f32[256,31]{0,1:T(8,128)S(1)} %stack.127, f32[256]{0:T(256)S(1)} %get-tuple-element.55), channel_id=1, replica_groups=mesh['ctx'=8,'exp'=4] {'ctx'}, use_global_device_ids=true, to_apply=%region_44.45 | all-reduce | flops 8192 | bytes 65536 | tf_op jit(solution)/shard_map/psum | solution.py:147
  (191 shorter events, 18.3 us)
Async XLA Ops:
  7.2 78.0 %copy-start = (bf16[1,1024,1024]{2,1,0:T(8,128)(2,1)S(1)}, bf16[1,1024,1024]{2,1,0:T(8,128)(2,1)}, u32[]{:S(2)}) copy-start(bf16[1,1024,1024]{2,1,0:T(8,128)(2,1)} %param.14) | copy-start | bytes 6291460
  8.3 32.8 %collective-permute-start = (bf16[256,15]{0,1:T(8,128)(2,1)S(1)}, bf16[256,15]{0,1:T(8,128)(2,1)S(1)}, u32[]{:S(2)}, u32[]{:S(2)}) collective-permute-start(bf16[256,15]{0,1:T(8,128)(2,1)S(1)} %get-tuple-element.71), channel_id=1, source_target_pairs={{0,4},{4,8},{8,12},{12,16},{16,20},{20,24},{24,28},{28,0},{1,5},{5... | collective-permute-start | bytes 23048 | tf_op jit(solution)/shard_map/ppermute | solution.py:16
  10.9 30.1 %collective-permute-start.1 = (bf16[256,15]{0,1:T(8,128)(2,1)S(1)}, bf16[256,15]{0,1:T(8,128)(2,1)S(1)}, u32[]{:S(2)}, u32[]{:S(2)}) collective-permute-start(bf16[256,15]{0,1:T(8,128)(2,1)S(1)} %get-tuple-element.72), channel_id=1, source_target_pairs={{4,0},{8,4},{12,8},{16,12},{20,16},{24,20},{28,24},{0,28},{5,1},{9... | collective-permute-start | bytes 23048 | tf_op jit(solution)/shard_map/ppermute | solution.py:18
  32.4 34.4 %all-to-all-start.2 = ((bf16[8,32,1024]{2,1,0:T(8,128)(2,1)}), bf16[8,32,1024]{2,1,0:T(8,128)(2,1)}, u32[]{:S(2)}, u32[]{:S(2)}) async-start(bf16[8,32,1024]{2,1,0:T(8,128)(2,1)} %bitcast.149), calls=%async_computation.3 | async-start | bytes 1048576 | tf_op jit(solution)/shard_map/all_to_all | solution.py:91
  66.8 15.8 %all-to-all-start = ((bf16[8,32,1024]{2,1,0:T(8,128)(2,1)}), bf16[8,32,1024]{2,1,0:T(8,128)(2,1)S(1)}, u32[]{:S(2)}, u32[]{:S(2)}) async-start(bf16[8,32,1024]{2,1,0:T(8,128)(2,1)} %bitcast.36), calls=%async_computation | async-start | bytes 1048576 | tf_op jit(solution)/shard_map/all_to_all | solution.py:90
  89.5 13.2 %all-to-all-start.1 = ((bf16[8,32,1024]{2,1,0:T(8,128)(2,1)}), bf16[8,32,1024]{2,1,0:T(8,128)(2,1)S(1)}, u32[]{:S(2)}, u32[]{:S(2)}) async-start(bf16[8,32,1024]{2,1,0:T(8,128)(2,1)} %fusion.15), calls=%async_computation.1 | async-start | bytes 1048576 | tf_op jit(solution)/shard_map/all_to_all | solution.py:43
  102.7 18.9 %all-to-all-start.3 = ((bf16[8,32,1024]{2,1,0:T(8,128)(2,1)}), bf16[8,32,1024]{2,1,0:T(8,128)(2,1)}, u32[]{:S(2)}, u32[]{:S(2)}) async-start(bf16[8,32,1024]{2,1,0:T(8,128)(2,1)} %bitcast.48), calls=%async_computation.4 | async-start | bytes 1048576 | tf_op jit(solution)/shard_map/all_to_all | solution.py:43
  109.7 26.8 %reduce-scatter.3.cloned.1.call-start = ((), (), s32[]{:S(2)}) async-start(), calls=%async_computation.6 | async-start | bytes 327680 | tf_op jit(solution)/shard_map/reduce_scatter | solution.py:52
  119.3 36.6 %reduce-scatter.5.cloned.1.call-start = ((), (), s32[]{:S(2)}) async-start(), calls=%async_computation.7 | async-start | bytes 327680 | tf_op jit(solution)/shard_map/reduce_scatter | solution.py:52
  132.9 37.4 %copy-start.65 = (f32[128]{0:T(128)S(1)}, f32[128]{0:T(128)}, u32[]{:S(2)}) copy-start(f32[128]{0:T(128)} %copy-done.64) | copy-start | bytes 1540
  170.4 32.5 %copy-start.19 = (f32[256,1]{0,1:T(1,128)S(1)}, f32[256,1]{0,1:T(1,128)}, u32[]{:S(2)}) copy-start(f32[256,1]{0,1:T(1,128)} %copy-done.18) | copy-start | bytes 3076
  170.4 32.5 %copy-start.21 = (f32[256,1]{0,1:T(1,128)S(1)}, f32[256,1]{0,1:T(1,128)}, u32[]{:S(2)}) copy-start(f32[256,1]{0,1:T(1,128)} %copy-done.20) | copy-start | bytes 3076
  170.4 32.5 %copy-start.23 = (f32[256,1]{0,1:T(1,128)S(1)}, f32[256,1]{0,1:T(1,128)}, u32[]{:S(2)}) copy-start(f32[256,1]{0,1:T(1,128)} %copy-done.22) | copy-start | bytes 3076
  170.4 32.5 %copy-start.25 = (f32[256,1]{0,1:T(1,128)S(1)}, f32[256,1]{0,1:T(1,128)}, u32[]{:S(2)}) copy-start(f32[256,1]{0,1:T(1,128)} %copy-done.24) | copy-start | bytes 3076
  170.4 32.5 %copy-start.27 = (f32[256,1]{0,1:T(1,128)S(1)}, f32[256,1]{0,1:T(1,128)}, u32[]{:S(2)}) copy-start(f32[256,1]{0,1:T(1,128)} %copy-done.26) | copy-start | bytes 3076
  170.4 32.5 %copy-start.29 = (f32[256,1]{0,1:T(1,128)S(1)}, f32[256,1]{0,1:T(1,128)}, u32[]{:S(2)}) copy-start(f32[256,1]{0,1:T(1,128)} %copy-done.28) | copy-start | bytes 3076
  170.4 32.5 %copy-start.31 = (f32[256,1]{0,1:T(1,128)S(1)}, f32[256,1]{0,1:T(1,128)}, u32[]{:S(2)}) copy-start(f32[256,1]{0,1:T(1,128)} %copy-done.30) | copy-start | bytes 3076
  170.5 32.5 %copy-start.33 = (f32[256,1]{0,1:T(1,128)S(1)}, f32[256,1]{0,1:T(1,128)}, u32[]{:S(2)}) copy-start(f32[256,1]{0,1:T(1,128)} %copy-done.32) | copy-start | bytes 3076
  170.5 32.5 %copy-start.35 = (f32[256,1]{0,1:T(1,128)S(1)}, f32[256,1]{0,1:T(1,128)}, u32[]{:S(2)}) copy-start(f32[256,1]{0,1:T(1,128)} %copy-done.34) | copy-start | bytes 3076
  170.5 32.5 %copy-start.37 = (f32[256,1]{0,1:T(1,128)S(1)}, f32[256,1]{0,1:T(1,128)}, u32[]{:S(2)}) copy-start(f32[256,1]{0,1:T(1,128)} %copy-done.36) | copy-start | bytes 3076
  170.5 32.5 %copy-start.39 = (f32[256,1]{0,1:T(1,128)S(1)}, f32[256,1]{0,1:T(1,128)}, u32[]{:S(2)}) copy-start(f32[256,1]{0,1:T(1,128)} %copy-done.38) | copy-start | bytes 3076
  170.5 32.5 %copy-start.41 = (f32[256,1]{0,1:T(1,128)S(1)}, f32[256,1]{0,1:T(1,128)}, u32[]{:S(2)}) copy-start(f32[256,1]{0,1:T(1,128)} %copy-done.40) | copy-start | bytes 3076
  170.5 32.5 %copy-start.43 = (f32[256,1]{0,1:T(1,128)S(1)}, f32[256,1]{0,1:T(1,128)}, u32[]{:S(2)}) copy-start(f32[256,1]{0,1:T(1,128)} %copy-done.42) | copy-start | bytes 3076
  170.5 32.5 %copy-start.45 = (f32[256,1]{0,1:T(1,128)S(1)}, f32[256,1]{0,1:T(1,128)}, u32[]{:S(2)}) copy-start(f32[256,1]{0,1:T(1,128)} %copy-done.44) | copy-start | bytes 3076
  170.5 32.5 %copy-start.47 = (f32[256,1]{0,1:T(1,128)S(1)}, f32[256,1]{0,1:T(1,128)}, u32[]{:S(2)}) copy-start(f32[256,1]{0,1:T(1,128)} %copy-done.46) | copy-start | bytes 3076
  170.5 32.5 %copy-start.49 = (f32[256,1]{0,1:T(1,128)S(1)}, f32[256,1]{0,1:T(1,128)}, u32[]{:S(2)}) copy-start(f32[256,1]{0,1:T(1,128)} %copy-done.48) | copy-start | bytes 3076
  170.5 32.5 %copy-start.51 = (f32[256,1]{0,1:T(1,128)S(1)}, f32[256,1]{0,1:T(1,128)}, u32[]{:S(2)}) copy-start(f32[256,1]{0,1:T(1,128)} %copy-done.50) | copy-start | bytes 3076
  170.6 32.5 %copy-start.53 = (f32[256,1]{0,1:T(1,128)S(1)}, f32[256,1]{0,1:T(1,128)}, u32[]{:S(2)}) copy-start(f32[256,1]{0,1:T(1,128)} %copy-done.52) | copy-start | bytes 3076
  170.6 32.5 %copy-start.55 = (f32[256,1]{0,1:T(1,128)S(1)}, f32[256,1]{0,1:T(1,128)}, u32[]{:S(2)}) copy-start(f32[256,1]{0,1:T(1,128)} %copy-done.54) | copy-start | bytes 3076
  170.6 32.5 %copy-start.57 = (f32[256,1]{0,1:T(1,128)S(1)}, f32[256,1]{0,1:T(1,128)}, u32[]{:S(2)}) copy-start(f32[256,1]{0,1:T(1,128)} %copy-done.56) | copy-start | bytes 3076
  172.0 30.9 %collective-permute-start.2 = (bf16[256,15]{0,1:T(8,128)(2,1)S(1)}, bf16[256,15]{0,1:T(8,128)(2,1)S(1)}, u32[]{:S(2)}, u32[]{:S(2)}) collective-permute-start(bf16[256,15]{0,1:T(8,128)(2,1)S(1)} %get-tuple-element.68), channel_id=1, source_target_pairs={{0,4},{4,8},{8,12},{12,16},{16,20},{20,24},{24,28},{28,0},{1,5},{5... | collective-permute-start | bytes 23048 | tf_op jit(solution)/shard_map/ppermute | solution.py:16
  179.2 23.7 %collective-permute-start.3 = (bf16[256,15]{0,1:T(8,128)(2,1)S(1)}, bf16[256,15]{0,1:T(8,128)(2,1)S(1)}, u32[]{:S(2)}, u32[]{:S(2)}) collective-permute-start(bf16[256,15]{0,1:T(8,128)(2,1)S(1)} %get-tuple-element.69), channel_id=1, source_target_pairs={{4,0},{8,4},{12,8},{16,12},{20,16},{24,20},{28,24},{0,28},{5,1},{9... | collective-permute-start | bytes 23048 | tf_op jit(solution)/shard_map/ppermute | solution.py:18
  (44 other events, 215.2 us)
Sparse Core Ops, SparseCore 0:
  119.4 16.1 reduce-scatter.2
  138.0 17.8 reduce-scatter.4
where the time goes:
time: 215 us; the launch traced here: 211 us
  blocking collectives  68 us (32%)
  starting transfers between devices  40.8 us (19%)
  waiting for transfers between devices  24.7 us (11%)
  local copies, waits for them, and re-layouts  24.1 us (11%)
  matrix products  20.8 us (10%)
  other arithmetic  17.6 us (8%)
  between operations  15.1 us (7%)
    psum x1, blocking collectives, local(): grad_taps, grad_gain = lax.psum((tap_local, gain_local), 'ctx')  22.2 us
    reduce_scatter x2, waiting for transfers between devices, bring_back(): lax.psum_scatter(term.astype(jnp.bfloat16), 'exp', scatter_dimension=1, t...  19.4 us
    all_to_all x2, starting transfers between devices, bring_back(): lax.all_to_all(values.reshape(experts, capacity, width).astype(jnp.bfloat...  13.5 us
    psum x1, blocking collectives, local(): lax.psum(jnp.sum(d_normed * gain_f[:, None] * mixed_f, axis=0), 'exp')  13.4 us
    all_gather x1, blocking collectives, local(): lax.all_gather(grad_out, 'exp', axis=0, tiled=True)  11.5 us
    all_gather x1, blocking collectives, local(): lax.all_gather(normed_part, 'exp', axis=0, tiled=True)  11 us
    psum x1, blocking collectives, local(): squares = lax.psum(jnp.sum(mixed_f * mixed_f, axis=0), 'exp')  9.88 us
    ppermute x2, starting transfers between devices, padded_2(): lax.ppermute(tail, axis, [(i, (i + 1) % count) for i in range(count)])  9.83 us
  transfers between devices with their start and end apart: 10, of which 3 were waited for; matrix products, arithmetic and copies ran while one was open for 24% of the time, Pallas kernels for 0%

commit v1 on v0

v1 whole, which is shorter than its diff:
```python
import functools
import jax
import jax.numpy as jnp
from jax import lax
from jax.experimental import pallas as pl
from jax.experimental.pallas import tpu as pltpu
from jax.sharding import PartitionSpec as P

EPS = 1e-05
MESH = pl.DeviceIdType.MESH
F32, BF16 = jnp.float32, jnp.bfloat16
LAST = (((1,), (1,)), ((), ()))
FIRST = (((0,), (0,)), ((), ()))


def greet(n, m):
    c, e = lax.axis_index("ctx"), lax.axis_index("exp")
    barrier = pltpu.get_barrier_semaphore()

    def ctx_peer(k, _):
        pl.semaphore_signal(barrier, inc=1, device_id=(lax.rem(c + k, n), e), device_id_type=MESH)
        return 0

    def exp_peer(k, _):
        pl.semaphore_signal(barrier, inc=1, device_id=(c, lax.rem(e + k, m)), device_id_type=MESH)
        return 0

    lax.fori_loop(1, n, ctx_peer, 0)
    lax.fori_loop(1, m, exp_peer, 0)
    pl.semaphore_wait(barrier, n + m - 2)


class Exchange:
    def __init__(self, axis, size, src, dst, send, recv):
        self.axis, self.size, self.src, self.dst = axis, size, src, dst
        self.send, self.recv = send, recv
        self.me = lax.axis_index(axis)

    def to(self, k):
        peer = lax.rem(self.me + k, self.size)
        if self.axis == "ctx":
            where = (peer, lax.axis_index("exp"))
        else:
            where = (lax.axis_index("ctx"), peer)
        return pltpu.make_async_remote_copy(
            src_ref=self.src(peer),
            dst_ref=self.dst(self.me),
            send_sem=self.send.at[peer],
            recv_sem=self.recv.at[self.me],
            device_id=where,
            device_id_type=MESH,
        )

    def frm(self, k):
        peer = lax.rem(self.me + k, self.size)
        if self.axis == "ctx":
            where = (peer, lax.axis_index("exp"))
        else:
            where = (lax.axis_index("ctx"), peer)
        return pltpu.make_async_remote_copy(
            src_ref=self.src(peer),
            dst_ref=self.dst(peer),
            send_sem=self.send.at[peer],
            recv_sem=self.recv.at[peer],
            device_id=where,
            device_id_type=MESH,
        )

    def each(self, act):
        def body(k, _):
            act(k)
            return 0

        lax.fori_loop(1, self.size, body, 0)

    def start(self):
        self.each(lambda k: self.to(k).start())

    def arrive(self):
        self.each(lambda k: self.frm(k).wait_recv())

    def sent(self):
        self.each(lambda k: self.to(k).wait_send())


class Halo:
    def __init__(self, n, block, left, right, sems):
        c, e = lax.axis_index("ctx"), lax.axis_index("exp")
        up, down = lax.rem(c + 1, n), lax.rem(c + n - 1, n)
        make = pltpu.make_async_remote_copy
        self.copies = [
            make(block, left, sems.at[0], sems.at[1], device_id=(up, e), device_id_type=MESH),
            make(block, right, sems.at[2], sems.at[3], device_id=(down, e), device_id_type=MESH),
        ]

    def start(self):
        for copy in self.copies:
            copy.start()

    def arrive(self):
        for copy in self.copies:
            copy.wait_recv()

    def sent(self):
        for copy in self.copies:
            copy.wait_send()


def shifted(block, left, right, offset, lane):
    width = block.shape[1]
    if offset == 0:
        return block
    if offset > 0:
        return pltpu.roll(jnp.where(lane >= offset, block, right), width - offset, axis=1)
    return pltpu.roll(jnp.where(lane < width + offset, block, left), -offset, axis=1)


def picks(aux, capacity, slots):
    tokens = aux.shape[0]
    lanes = lax.broadcasted_iota(jnp.int32, (tokens, 128), 1)
    named = [aux[:, k : k + 1].astype(jnp.int32) for k in range(2)]
    hot = [(lanes == r).astype(F32) for r in named]
    row = lax.broadcasted_iota(jnp.int32, (tokens, tokens), 0)
    col = lax.broadcasted_iota(jnp.int32, (tokens, tokens), 1)
    earlier = (col < row).astype(F32).astype(BF16)
    count = jnp.dot(earlier, (hot[0] + hot[1]).astype(BF16), preferred_element_type=F32)
    place = lax.broadcasted_iota(jnp.int32, (tokens, slots), 1)
    out = []
    for r, h in zip(named, hot):
        slot = jnp.sum(count * h, axis=1, keepdims=True).astype(jnp.int32)
        out.append((place == r * capacity + slot).astype(F32))
    return out


def front(n, m, taps, capacity, x_ref, pack_ref, aux_ref, cot_ref,
          rx_ref, rdy_ref, mixed_ref, scale_ref, left_ref, right_ref, cots_ref,
          nrm, sq, sx, sdy, hs, cs, cr, qs, qr, ns, nr, ys, yr, xs, xr):
    me, mine = lax.axis_index("ctx"), lax.axis_index("exp")
    chans, tokens = x_ref.shape
    slots, width = sx.shape
    half = taps // 2
    greet(n, m)
    halo = Halo(n, x_ref, left_ref, right_ref, hs)
    halo.start()
    gather_cot = Exchange("exp", m, lambda p: cot_ref, lambda s: cots_ref.at[s], cs, cr)
    gather_cot.start()
    cots_ref[mine] = cot_ref[...]
    aux = aux_ref[...]
    p0, p1 = picks(aux, capacity, slots)
    pt = jnp.transpose(p0 + p1).astype(BF16)
    gated = jnp.transpose(p0 * aux[:, 2:3] + p1 * aux[:, 3:4])
    gate = jnp.sum(gated, axis=1, keepdims=True)

    halo.arrive()
    x = x_ref[...].astype(F32)
    left, right = left_ref[...].astype(F32), right_ref[...].astype(F32)
    pack = pack_ref[...]
    lane = lax.broadcasted_iota(jnp.int32, (chans, tokens), 1)
    conv = jnp.zeros((chans, tokens), F32)
    for j in range(taps):
        conv = conv + pack[:, j : j + 1] * shifted(x, left, right, j - half, lane)
    mixed = (x + conv).astype(BF16)
    mixed_ref[...] = mixed
    mixed = mixed.astype(F32)
    sq[mine] = jnp.broadcast_to(jnp.sum(mixed * mixed, axis=0, keepdims=True), (8, tokens))
    squares = Exchange("exp", m, lambda p: sq.at[mine], lambda s: sq.at[s], qs, qr)
    squares.start()

    def rows(ref):
        return lambda p: ref.at[pl.ds(pl.multiple_of(p * capacity, capacity), capacity)]

    own = pl.ds(pl.multiple_of(me * capacity, capacity), capacity)
    gather_cot.arrive()
    for k in range(m):
        part = lax.dot_general(pt, cots_ref[k], LAST, preferred_element_type=F32)
        sdy[:, k * chans : (k + 1) * chans] = (part * gate).astype(BF16)
    send_dy = Exchange("ctx", n, rows(sdy), rows(rdy_ref), ys, yr)
    squares.arrive()
    total = jnp.sum(sq[...], axis=0)
    scale = lax.rsqrt(total / width + EPS)
    scale_ref[...] = scale
    nrm[mine] = (mixed * pack[:, taps : taps + 1] * scale[:1]).astype(BF16)
    gather_x = Exchange("exp", m, lambda p: nrm.at[mine], lambda s: nrm.at[s], ns, nr)
    gather_x.start()
    send_dy.start()
    rdy_ref[own, :] = sdy[own, :]
    gather_x.arrive()
    for k in range(m):
        part = lax.dot_general(pt, nrm[k], LAST, preferred_element_type=F32)
        sx[:, k * chans : (k + 1) * chans] = part.astype(BF16)
    send_x = Exchange("ctx", n, rows(sx), rows(rx_ref), xs, xr)
    send_x.start()
    rx_ref[own, :] = sx[own, :]
    send_dy.arrive()
    send_x.arrive()
    for done in (halo, gather_cot, squares, send_dy, gather_x, send_x):
        done.sent()


def back(n, m, taps, capacity, y_ref, dx_ref, x_ref, left_ref, right_ref, pack_ref, aux_ref, cot_ref,
         cots_ref, mixed_ref, scale_ref,
         out_ref, gin_ref, tap_ref, gg_ref,
         by, bdx, zdx, zy, rdx, ry, dots, norm, dm, dl, dr, tp,
         ds_, dr_, ys, yr, as_, ar, bs, br, gs, gr, qs, qr, hs, ts, tr):
    me, mine = lax.axis_index("ctx"), lax.axis_index("exp")
    chans, tokens = x_ref.shape
    slots, width = by.shape
    half = taps // 2
    greet(n, m)

    def rows(ref):
        return lambda p: ref.at[pl.ds(pl.multiple_of(p * capacity, capacity), capacity)]

    own = pl.ds(pl.multiple_of(me * capacity, capacity), capacity)
    send_dx = Exchange("ctx", n, rows(dx_ref), rows(bdx), ds_, dr_)
    send_y = Exchange("ctx", n, rows(y_ref), rows(by), ys, yr)
    send_dx.start()
    send_y.start()
    bdx[own, :] = dx_ref[own, :]
    by[own, :] = y_ref[own, :]
    aux = aux_ref[...]
    p0, p1 = picks(aux, capacity, slots)
    both = (p0 + p1).astype(BF16)
    p0, p1 = p0.astype(BF16), p1.astype(BF16)
    x = x_ref[...].astype(F32)
    left, right = left_ref[...].astype(F32), right_ref[...].astype(F32)
    mixed = mixed_ref[...].astype(F32)
    pack = pack_ref[...]
    gain = pack[:, taps : taps + 1]
    scale = scale_ref[:1]
    cot = cot_ref[...].astype(F32)

    send_dx.arrive()
    for k in range(m):
        part = jnp.dot(both, bdx[:, k * chans : (k + 1) * chans], preferred_element_type=F32)
        zdx[k] = part.astype(BF16)
    sum_dx = Exchange("exp", m, lambda p: zdx.at[p], lambda s: rdx.at[s], as_, ar)
    sum_dx.start()
    rdx[mine] = zdx[mine]
    send_y.arrive()
    d0 = jnp.zeros((tokens, 1), F32)
    d1 = jnp.zeros((tokens, 1), F32)
    for k in range(m):
        block = by[:, k * chans : (k + 1) * chans]
        y0 = jnp.dot(p0, block, preferred_element_type=F32)
        y1 = jnp.dot(p1, block, preferred_element_type=F32)
        zy[k] = (y0 * aux[:, 2:3] + y1 * aux[:, 3:4]).astype(BF16)
        turned = jnp.transpose(cots_ref[k].astype(F32))
        d0 = d0 + jnp.sum(y0 * turned, axis=1, keepdims=True)
        d1 = d1 + jnp.sum(y1 * turned, axis=1, keepdims=True)
    sum_y = Exchange("exp", m, lambda p: zy.at[p], lambda s: ry.at[s], bs, br)
    sum_y.start()
    ry[mine] = zy[mine]
    col = lax.broadcasted_iota(jnp.int32, (tokens, 128), 1)
    dots[mine] = jnp.transpose(jnp.where(col == 0, d0, jnp.where(col == 1, d1, 0.0)))[:8]
    sum_dots = Exchange("exp", m, lambda p: dots.at[mine], lambda s: dots.at[s], gs, gr)
    sum_dots.start()

    sum_dx.arrive()
    dn = jnp.transpose(jnp.sum(rdx[...].astype(F32), axis=0))
    weighted = dn * mixed
    norm[mine] = jnp.broadcast_to(jnp.sum(weighted * gain, axis=0, keepdims=True), (8, tokens))
    sum_norm = Exchange("exp", m, lambda p: norm.at[mine], lambda s: norm.at[s], qs, qr)
    sum_norm.start()
    lane = lax.broadcasted_iota(jnp.int32, (chans, tokens), 1)
    gain_grad = jnp.sum(weighted * scale, axis=1, keepdims=True)
    sum_norm.arrive()
    q = jnp.sum(norm[...], axis=0)[:1]
    d_mixed = cot + gain * dn * scale - mixed * (q * scale * scale * scale / width)
    dm[...] = d_mixed.astype(BF16)
    halo = Halo(n, dm, dl, dr, hs)
    halo.start()
    grads = jnp.where(lane == taps, gain_grad, 0.0)
    for j in range(taps):
        term = jnp.sum(d_mixed * shifted(x, left, right, j - half, lane), axis=1, keepdims=True)
        grads = jnp.where(lane == j, term, grads)
    tp[me] = jnp.transpose(grads)[: tp.shape[1]]
    sum_taps = Exchange("ctx", n, lambda p: tp.at[me], lambda s: tp.at[s], ts, tr)
    sum_taps.start()
    halo.arrive()
    dleft, dright = dl[...].astype(F32), dr[...].astype(F32)
    grad = d_mixed
    for j in range(taps):
        grad = grad + pack[:, j : j + 1] * shifted(d_mixed, dleft, dright, half - j, lane)
    gin_ref[...] = grad.astype(BF16)
    sum_y.arrive()
    out_ref[...] = (mixed + jnp.transpose(jnp.sum(ry[...].astype(F32), axis=0))).astype(BF16)
    sum_dots.arrive()
    gg_ref[...] = jnp.sum(dots[...], axis=0)
    sum_taps.arrive()
    tap_ref[...] = jnp.sum(tp[...], axis=0)
    for done in (send_dx, send_y, sum_dx, sum_y, sum_dots, sum_norm, halo, sum_taps):
        done.sent()


def sems(*counts):
    out = []
    for count in counts:
        out += [pltpu.SemaphoreType.DMA((count,)), pltpu.SemaphoreType.DMA((count,))]
    return out


def local(inputs, conv_taps, norm_gain, routes, gate_probs, w_gate, w_up, w_down, grad_out):
    chans, tokens = inputs.shape
    taps = conv_taps.shape[1]
    width = w_gate.shape[1]
    n, m = lax.axis_size("ctx"), lax.axis_size("exp")
    capacity = max(tokens // 8, (2 * tokens + n - 1) // n)
    slots = n * capacity
    pad = -(-(taps + 1) // 8) * 8
    pack = jnp.concatenate([conv_taps, norm_gain.astype(F32)[:, None]], axis=1)
    aux = jnp.concatenate([routes.astype(F32), gate_probs], axis=1)
    vmem = pl.BlockSpec(memory_space=pltpu.VMEM)
    shape = jax.ShapeDtypeStruct
    rx, rdy, mixed, scale, left, right, cots = pl.pallas_call(
        functools.partial(front, n, m, taps, capacity),
        out_shape=(
            shape((slots, width), BF16),
            shape((slots, width), BF16),
            shape((chans, tokens), BF16),
            shape((8, tokens), F32),
            shape((chans, tokens), BF16),
            shape((chans, tokens), BF16),
            shape((m, chans, tokens), BF16),
        ),
        in_specs=[vmem] * 4,
        out_specs=(vmem,) * 7,
        scratch_shapes=[
            pltpu.VMEM((m, chans, tokens), BF16),
            pltpu.VMEM((m, 8, tokens), F32),
            pltpu.VMEM((slots, width), BF16),
            pltpu.VMEM((slots, width), BF16),
            pltpu.SemaphoreType.DMA((4,)),
            *sems(m, m, m, n, n),
        ],
        compiler_params=pltpu.CompilerParams(
            collective_id=0, has_side_effects=True, vmem_limit_bytes=40 << 20
        ),
        name="front",
    )(inputs, pack, aux, grad_out)
    weight_gate, weight_up, weight_down = w_gate[0], w_up[0], w_down[0]
    gate_act = jnp.dot(rx, weight_gate, preferred_element_type=F32)
    up_act = jnp.dot(rx, weight_up, preferred_element_type=F32)
    sigma = jax.nn.sigmoid(gate_act)
    hidden = (gate_act * sigma * up_act).astype(BF16)
    result = jnp.dot(hidden, weight_down, preferred_element_type=F32).astype(BF16)
    d_hidden = lax.dot_general(rdy, weight_down, LAST, preferred_element_type=F32)
    d_gate = (d_hidden * up_act * sigma * (1.0 + gate_act * (1.0 - sigma))).astype(BF16)
    d_up = (d_hidden * gate_act * sigma).astype(BF16)
    d_rows = lax.dot_general(d_gate, weight_gate, LAST, preferred_element_type=F32)
    d_rows = d_rows + lax.dot_general(d_up, weight_up, LAST, preferred_element_type=F32)
    d_rows = d_rows.astype(BF16)
    grad_down = lax.dot_general(hidden, rdy, FIRST, preferred_element_type=F32).astype(BF16)
    grad_gate = lax.dot_general(rx, d_gate, FIRST, preferred_element_type=F32).astype(BF16)
    grad_up = lax.dot_general(rx, d_up, FIRST, preferred_element_type=F32).astype(BF16)
    layer_out, grad_in, tap_sum, gate_sum = pl.pallas_call(
        functools.partial(back, n, m, taps, capacity),
        out_shape=(
            shape((chans, tokens), BF16),
            shape((chans, tokens), BF16),
            shape((pad, chans), F32),
            shape((8, tokens), F32),
        ),
        in_specs=[vmem] * 11,
        out_specs=(vmem,) * 4,
        scratch_shapes=[
            pltpu.VMEM((slots, width), BF16),
            pltpu.VMEM((slots, width), BF16),
            pltpu.VMEM((m, tokens, chans), BF16),
            pltpu.VMEM((m, tokens, chans), BF16),
            pltpu.VMEM((m, tokens, chans), BF16),
            pltpu.VMEM((m, tokens, chans), BF16),
            pltpu.VMEM((m, 8, tokens), F32),
            pltpu.VMEM((m, 8, tokens), F32),
            pltpu.VMEM((chans, tokens), BF16),
            pltpu.VMEM((chans, tokens), BF16),
            pltpu.VMEM((chans, tokens), BF16),
            pltpu.VMEM((n, pad, chans), F32),
            *sems(n, n, m, m, m, m),
            pltpu.SemaphoreType.DMA((4,)),
            *sems(n),
        ],
        compiler_params=pltpu.CompilerParams(
            collective_id=1, has_side_effects=True, vmem_limit_bytes=40 << 20
        ),
        name="back",
    )(result, d_rows, inputs, left, right, pack, aux, grad_out, cots, mixed, scale)
    return (
        layer_out,
        grad_in,
        tap_sum[:taps].T,
        tap_sum[taps],
        gate_sum[:2].T,
        grad_gate[None],
        grad_up[None],
        grad_down[None],
    )


def solution(mesh):
    return jax.shard_map(
        local,
        mesh=mesh,
        in_specs=(
            P("exp", "ctx"),
            P("exp", None),
            P("exp"),
            P("ctx", None),
            P("ctx", None),
            P("ctx", None, "exp"),
            P("ctx", None, "exp"),
            P("ctx", "exp", None),
            P("exp", "ctx"),
        ),
        out_specs=(
            P("exp", "ctx"),
            P("exp", "ctx"),
            P("exp", None),
            P("exp"),
            P("ctx", None),
            P("ctx", None, "exp"),
            P("ctx", None, "exp"),
            P("ctx", "exp", None),
        ),
        check_vma=False,
    )
```

time: 215 us -> 85.2 us (0.40); the launches traced: 211 us -> 84.8 us
  blocking collectives: 68 us -> 0 us
  Pallas kernels: 0 us -> 63.1 us
  starting transfers between devices: 40.8 us -> 0 us
  waiting for transfers between devices: 24.7 us -> 0 us
  local copies, waits for them, and re-layouts: 24.1 us -> 5.29 us
  other arithmetic: 17.6 us -> 2.94 us
  between operations: 15.1 us -> 0.74 us
  matrix products: 20.8 us -> 12.8 us
    pallas_call x0 -> x2, Pallas kernels: none -> 63.1 us  [the longest x1 35.3 us: local(): pl.pallas_call(functools.partial(back, n, m, taps, capacity), out_shape=(...]
    psum x3 -> x0, blocking collectives: 45.5 us -> none  [the longest x1 22.2 us: local(): grad_taps, grad_gain = lax.psum((tap_local, gain_local), 'ctx')]
    all_to_all x4 -> x0, starting transfers between devices: 30.9 us -> none  [the longest x2 13.5 us: bring_back(): lax.all_to_all(values.reshape(experts, capacity, width).astype(jnp.bfloat...]
    all_gather x2 -> x0, blocking collectives: 22.5 us -> none  [the longest x1 11.5 us: local(): lax.all_gather(grad_out, 'exp', axis=0, tiled=True)]
    reduce_scatter x2 -> x0, waiting for transfers between devices: 19.4 us -> none  [bring_back(): lax.psum_scatter(term.astype(jnp.bfloat16), 'exp', scatter_dimension=1, t...]
    reduce_sum x8 -> x0, other arithmetic: 10.2 us -> none  [the longest x2 6.53 us: bring_back(): term = jnp.sum((picked * weights[:, None]).reshape(-1, 2, width), axis=1)]
    ppermute x4 -> x0, starting transfers between devices: 9.84 us -> none  [the longest x2 9.83 us: padded_2(): lax.ppermute(tail, axis, [(i, (i + 1) % count) for i in range(count)])]
    dot_general x9, matrix products: 20.8 us -> 12.8 us  [the longest x1 2.39 us: local(): lax.dot_general(rdy, weight_down, LAST, preferred_element_type=F32)]
  transfers between devices with their start and end apart: 10 -> 0, of which waited for: 3 -> 0; matrix products, arithmetic and copies ran while one was open for 24% -> 0% of each run, Pallas kernels for 0% -> 0%
where the time goes in v1:
time: 85.2 us; the launch traced here: 84.8 us
  Pallas kernels  63.1 us (74%)
  matrix products  12.8 us (15%)
  local copies, waits for them, and re-layouts  5.29 us (6%)
  other arithmetic  2.94 us (3%)
    pallas_call x1, Pallas kernels, local(): pl.pallas_call(functools.partial(back, n, m, taps, capacity), out_shape=(...  35.3 us
    pallas_call x1, Pallas kernels, local(): pl.pallas_call(functools.partial(front, n, m, taps, capacity), out_shape=...  27.8 us
    unnamed x12, local copies, waits for them, and re-layouts  3.34 us
    dot_general x1, matrix products, local(): lax.dot_general(rdy, weight_down, LAST, preferred_element_type=F32)  2.39 us
    dot_general x1, matrix products, local(): lax.dot_general(hidden, rdy, FIRST, preferred_element_type=F32).astype(BF16)  2.07 us
    dot_general x1, matrix products, local(): lax.dot_general(rx, d_gate, FIRST, preferred_element_type=F32).astype(BF16)  2.07 us
    dot_general x1, matrix products, local(): lax.dot_general(rx, d_up, FIRST, preferred_element_type=F32).astype(BF16)  2.07 us

profile of v1, /device:TPU:1, one launch (start us, length us, event | category | flops | bytes accessed | tf_op | source)
XLA Modules:
  0.0 84.8 jit_solution(4032520844724396359)
XLA Ops:
  0.6 0.0 copy-start
  0.6 0.8 broadcast_in_dim.20
  1.5 0.7 convert_element_type.28
  2.1 0.7 pad_maximum_fusion.1
  2.8 0.8 pad_maximum_fusion
  3.6 0.1 copy.25.aux_ref
  3.7 0.1 copy.24.pack_ref
  3.8 0.0 copy-start.1
  3.8 0.8 copy-done.1
  4.6 0.0 copy-start.2
  4.6 0.8 copy-done.2
  5.5 0.0 copy-start.3
  5.5 27.8 %front.1 = (bf16[256,1024]{1,0:T(8,128)(2,1)S(1)}, bf16[256,1024]{1,0:T(8,128)(2,1)S(1)}, bf16[256,128]{1,0:T(8,128)(2,1)S(1)}, f32[8,128]{1,0:T(8,128)S(1)}, bf...) custom-call(bf16[256,128]{1,0:T(8,128)(2,1)S(1)} %copy-done.1, ...), custom_call_target="tpu_custom_call" | custom-call | tf_op jit(solution)/shard_map/front/pallas_call | solution.py:315
  33.3 2.4 %fusion = f32[256,1024]{1,0:T(8,128)S(1)} fusion(bf16[256,1024]{1,0:T(8,128)(2,1)S(1)} %get-tuple-element.20, bf16[1,1024,1024]{2,1,0:T(8,128)(2,1)} %param.16), kind=kOutput, calls=%fused_computation | convolution fusion | flops 536870912 | bytes 3670016 | tf_op jit(solution)/shard_map/dot_general | solution.py:347
  35.7 0.0 copy-done.3
  35.7 0.7 fusion.6
  36.5 0.0 copy-done
  36.5 0.0 copy-start.4
  36.5 1.2 %multiply_convert_fusion.1 = (bf16[256,1024]{1,0:T(8,128)(2,1)S(1)}, bf16[256,1024]{1,0:T(8,128)(2,1)S(1)}, bf16[256,1024]{1,0:T(8,128)(2,1)S(1)}) fusion(f32[256,1024]{1,0:T(8,128)S(1)} %fusion, f32[256,1024]{1,0:T(8,128)S(1)} %fusion.6, bf16[256,1024]{1,0:T(8,128)(2,1)S(1)} %get-tuple-element.19, bf16[1,1024,1024]{2,1,0:T(8,128)(2,1)S(1)} %copy-done), kind=kOutput, calls=%fused_computation.19 | convolution fusion | flops 541065216 | bytes 6291456 | tf_op jit(solution)/shard_map/dot_general | solution.py:342
  37.7 0.4 copy-done.4
  38.1 0.7 fusion.15.y_ref
  38.8 2.1 %convert_bitcast_fusion = bf16[1,1024,1024]{2,1,0:T(8,128)(2,1)} fusion(bf16[256,1024]{1,0:T(8,128)(2,1)S(1)} %get-tuple-element.31, bf16[256,1024]{1,0:T(8,128)(2,1)S(1)} %get-tuple-element.20), kind=kOutput, calls=%fused_computation.12 | convolution fusion | flops 537919488 | bytes 3145728 | tf_op jit(solution)/shard_map/dot_general | solution.py:353
  40.8 0.7 fusion.4
  41.6 0.8 fusion.18.dx_ref
  42.4 35.3 %back.1 = (bf16[256,128]{1,0:T(8,128)(2,1)S(1)}, bf16[256,128]{1,0:T(8,128)(2,1)S(1)}, f32[32,256]{1,0:T(8,128)S(1)}, f32[8,128]{1,0:T(8,128)S(1)}) custom-call(bf16[256,1024]{1,0:T(8,128)(2,1)S(1)} %fusion.15.y_ref, bf16[256,1024]{1,0:T(8,128)(2,1)S(1)} %fusion.18.dx_ref, bf16[256,128]{1,0:T(8,128)(2,1)S(1)} %copy-done.1, ...), custom_call_target="tpu_custom_call" | custom-call | tf_op jit(solution)/shard_map/back/pallas_call | solution.py:356
  77.7 0.6 slice_bitcast_fusion.1
  78.2 0.6 slice.10
  78.8 0.6 slice_bitcast_fusion
  79.4 2.1 %convert_bitcast_fusion.2 = bf16[1,1024,1024]{2,1,0:T(8,128)(2,1)} fusion(bf16[256,1024]{1,0:T(8,128)(2,1)S(1)} %get-tuple-element.19, bf16[256,1024]{1,0:T(8,128)(2,1)S(1)} %get-tuple-element.30), kind=kOutput, calls=%fused_computation.14 | convolution fusion | flops 537919488 | bytes 3145728 | tf_op jit(solution)/shard_map/dot_general | solution.py:354
  81.5 2.1 %convert_bitcast_fusion.1 = bf16[1,1024,1024]{2,1,0:T(8,128)(2,1)} fusion(bf16[256,1024]{1,0:T(8,128)(2,1)S(1)} %get-tuple-element.19, bf16[256,1024]{1,0:T(8,128)(2,1)S(1)} %get-tuple-element.32), kind=kOutput, calls=%fused_computation.13 | convolution fusion | flops 537919488 | bytes 3145728 | tf_op jit(solution)/shard_map/dot_general | solution.py:355
  83.6 0.6 copy.30
  84.2 0.6 copy.31
Async XLA Ops:
  0.6 35.8 %copy-start = (bf16[1,1024,1024]{2,1,0:T(8,128)(2,1)S(1)}, bf16[1,1024,1024]{2,1,0:T(8,128)(2,1)}, u32[]{:S(2)}) copy-start(bf16[1,1024,1024]{2,1,0:T(8,128)(2,1)} %param.14) | copy-start | bytes 6291460
  3.8 0.8 copy-start.1
  4.6 0.8 copy-start.2
  5.5 30.2 %copy-start.3 = (bf16[1,1024,1024]{2,1,0:T(8,128)(2,1)S(1)}, bf16[1,1024,1024]{2,1,0:T(8,128)(2,1)}, u32[]{:S(2)}) copy-start(bf16[1,1024,1024]{2,1,0:T(8,128)(2,1)} %param.15) | copy-start | bytes 6291460
  36.5 1.6 %copy-start.4 = (bf16[1,1024,1024]{2,1,0:T(8,128)(2,1)S(1)}, bf16[1,1024,1024]{2,1,0:T(8,128)(2,1)}, u32[]{:S(2)}) copy-start(bf16[1,1024,1024]{2,1,0:T(8,128)(2,1)} %param.16) | copy-start | bytes 6291460

commit v2 on v1

v2 whole, which is shorter than its diff:
```python
import functools
import jax
import jax.numpy as jnp
from jax import lax
from jax.experimental import pallas as pl
from jax.experimental.pallas import tpu as pltpu
from jax.sharding import PartitionSpec as P

EPS = 1e-05
MESH = pl.DeviceIdType.MESH
F32, BF16 = jnp.float32, jnp.bfloat16
LAST = (((1,), (1,)), ((), ()))
FIRST = (((0,), (0,)), ((), ()))


def greet(n, m):
    c, e = lax.axis_index("ctx"), lax.axis_index("exp")
    barrier = pltpu.get_barrier_semaphore()

    def ctx_peer(k, _):
        pl.semaphore_signal(barrier, inc=1, device_id=(lax.rem(c + k, n), e), device_id_type=MESH)
        return 0

    def exp_peer(k, _):
        pl.semaphore_signal(barrier, inc=1, device_id=(c, lax.rem(e + k, m)), device_id_type=MESH)
        return 0

    lax.fori_loop(1, n, ctx_peer, 0)
    lax.fori_loop(1, m, exp_peer, 0)
    pl.semaphore_wait(barrier, n + m - 2)


class Exchange:
    def __init__(self, axis, size, src, dst, send, recv):
        self.axis, self.size, self.src, self.dst = axis, size, src, dst
        self.send, self.recv = send, recv
        self.me = lax.axis_index(axis)

    def to(self, k):
        peer = lax.rem(self.me + k, self.size)
        if self.axis == "ctx":
            where = (peer, lax.axis_index("exp"))
        else:
            where = (lax.axis_index("ctx"), peer)
        return pltpu.make_async_remote_copy(
            src_ref=self.src(peer),
            dst_ref=self.dst(self.me),
            send_sem=self.send.at[peer],
            recv_sem=self.recv.at[self.me],
            device_id=where,
            device_id_type=MESH,
        )

    def frm(self, k):
        peer = lax.rem(self.me + k, self.size)
        if self.axis == "ctx":
            where = (peer, lax.axis_index("exp"))
        else:
            where = (lax.axis_index("ctx"), peer)
        return pltpu.make_async_remote_copy(
            src_ref=self.src(peer),
            dst_ref=self.dst(peer),
            send_sem=self.send.at[peer],
            recv_sem=self.recv.at[peer],
            device_id=where,
            device_id_type=MESH,
        )

    def each(self, act):
        def body(k, _):
            act(k)
            return 0

        lax.fori_loop(1, self.size, body, 0)

    def start(self):
        self.each(lambda k: self.to(k).start())

    def arrive(self):
        self.each(lambda k: self.frm(k).wait_recv())

    def sent(self):
        self.each(lambda k: self.to(k).wait_send())


class Halo:
    def __init__(self, n, block, left, right, sems):
        c, e = lax.axis_index("ctx"), lax.axis_index("exp")
        up, down = lax.rem(c + 1, n), lax.rem(c + n - 1, n)
        make = pltpu.make_async_remote_copy
        self.copies = [
            make(block, left, sems.at[0], sems.at[1], device_id=(up, e), device_id_type=MESH),
            make(block, right, sems.at[2], sems.at[3], device_id=(down, e), device_id_type=MESH),
        ]

    def start(self):
        for copy in self.copies:
            copy.start()

    def arrive(self):
        for copy in self.copies:
            copy.wait_recv()

    def sent(self):
        for copy in self.copies:
            copy.wait_send()


def shifted(block, left, right, offset, lane):
    width = block.shape[1]
    if offset == 0:
        return block
    if offset > 0:
        return pltpu.roll(jnp.where(lane >= offset, block, right), width - offset, axis=1)
    return pltpu.roll(jnp.where(lane < width + offset, block, left), -offset, axis=1)


def picks(routes, capacity, slots):
    tokens = routes.shape[1]
    names = lax.broadcasted_iota(jnp.int32, (128, tokens), 0)
    named = [routes[k : k + 1] for k in range(2)]
    hot = [(names == r).astype(F32) for r in named]
    row = lax.broadcasted_iota(jnp.int32, (tokens, tokens), 0)
    col = lax.broadcasted_iota(jnp.int32, (tokens, tokens), 1)
    earlier = (row < col).astype(F32).astype(BF16)
    count = jnp.dot((hot[0] + hot[1]).astype(BF16), earlier, preferred_element_type=F32)
    place = lax.broadcasted_iota(jnp.int32, (slots, tokens), 0)
    out = []
    for r, h in zip(named, hot):
        slot = jnp.sum(count * h, axis=0, keepdims=True).astype(jnp.int32)
        out.append((place == r * capacity + slot).astype(F32))
    return out


def columns(taps_ref, gain_ref, pad):
    taps, chans = taps_ref.shape
    gain = gain_ref[...].astype(F32)
    rows = [taps_ref[...], gain]
    if pad > taps + 1:
        rows.append(jnp.zeros((pad - taps - 1, chans), F32))
    return jnp.transpose(jnp.concatenate(rows, axis=0))


def parts(n, m, capacity, src, dst, send, recv):
    def rows(ref, k):
        return lambda p: ref.at[k, pl.ds(pl.multiple_of(p * capacity, capacity), capacity)]

    return [Exchange("ctx", n, rows(src, k), rows(dst, k), send.at[k], recv.at[k]) for k in range(m)]


def front(n, m, capacity, pad, x_ref, taps_ref, gain_ref, routes_ref, gates_ref, cot_ref,
          rx_ref, rdy_ref, mixed_ref, scale_ref, left_ref, right_ref, cots_ref,
          nrm, sq, sx, sdy, gx, gdy, hs, cs, cr, qs, qr, ns, nr, ys, yr, xs, xr):
    me, mine = lax.axis_index("ctx"), lax.axis_index("exp")
    chans, tokens = x_ref.shape
    slots, width = rx_ref.shape
    taps = taps_ref.shape[0]
    half = taps // 2
    greet(n, m)
    halo = Halo(n, x_ref, left_ref, right_ref, hs)
    halo.start()
    gather_cot = Exchange("exp", m, lambda p: cot_ref, lambda s: cots_ref.at[s], cs, cr)
    gather_cot.start()
    cots_ref[mine] = cot_ref[...]
    p0, p1 = picks(routes_ref[...], capacity, slots)
    pt = (p0 + p1).astype(BF16)
    gates = gates_ref[...]
    gate = jnp.sum(p0 * gates[:1] + p1 * gates[1:], axis=1, keepdims=True)
    pack = columns(taps_ref, gain_ref, pad)
    own = pl.ds(pl.multiple_of(me * capacity, capacity), capacity)

    halo.arrive()
    x = x_ref[...].astype(F32)
    left, right = left_ref[...].astype(F32), right_ref[...].astype(F32)
    lane = lax.broadcasted_iota(jnp.int32, (chans, tokens), 1)
    conv = jnp.zeros((chans, tokens), F32)
    for j in range(taps):
        conv = conv + pack[:, j : j + 1] * shifted(x, left, right, j - half, lane)
    mixed = (x + conv).astype(BF16)
    mixed_ref[...] = mixed
    mixed = mixed.astype(F32)
    sq[mine] = jnp.broadcast_to(jnp.sum(mixed * mixed, axis=0, keepdims=True), (8, tokens))
    squares = Exchange("exp", m, lambda p: sq.at[mine], lambda s: sq.at[s], qs, qr)
    squares.start()

    send_dy = parts(n, m, capacity, sdy, gdy, ys, yr)
    gather_cot.arrive()
    for k in range(m):
        part = lax.dot_general(pt, cots_ref[k], LAST, preferred_element_type=F32)
        sdy[k] = (part * gate).astype(BF16)
        send_dy[k].start()
        gdy[k, own] = sdy[k, own]
    squares.arrive()
    scale = lax.rsqrt(jnp.sum(sq[...], axis=0) / width + EPS)
    scale_ref[...] = scale
    nrm[mine] = (mixed * pack[:, taps : taps + 1] * scale[:1]).astype(BF16)
    gather_x = Exchange("exp", m, lambda p: nrm.at[mine], lambda s: nrm.at[s], ns, nr)
    gather_x.start()

    def part_of(k):
        k = lax.rem(mine + k, m)
        part = lax.dot_general(pt, nrm[k], LAST, preferred_element_type=F32)
        sx[k] = part.astype(BF16)
        rows = lambda ref: lambda p: ref.at[k, pl.ds(pl.multiple_of(p * capacity, capacity), capacity)]
        return Exchange("ctx", n, rows(sx), rows(gx), xs.at[k], xr.at[k]), k

    def forward(k):
        send, k = part_of(k)
        send.start()
        gx[k, own] = sx[k, own]

    forward(0)
    for k in range(1, m):
        gather_x.frm(k).wait_recv()
        forward(k)
    send_x = parts(n, m, capacity, sx, gx, xs, xr)
    for k in range(m):
        send_dy[k].arrive()
        rdy_ref[:, k * chans : (k + 1) * chans] = gdy[k]
    for k in range(m):
        send_x[k].arrive()
        rx_ref[:, k * chans : (k + 1) * chans] = gx[k]
    for done in (halo, gather_cot, squares, gather_x, *send_dy, *send_x):
        done.sent()


def grad_into(out_ref, lhs_ref, rhs_ref, tile):
    right = rhs_ref[...]

    def body(i, _):
        at = pl.ds(pl.multiple_of(i * tile, tile), tile)
        out_ref[at, :] = lax.dot_general(
            lhs_ref[:, at], right, FIRST, preferred_element_type=F32
        ).astype(BF16)
        return 0

    lax.fori_loop(0, lhs_ref.shape[1] // tile, body, 0)


def back(n, m, capacity, pad, y_ref, dx_ref, rx_ref, rdy_ref, hidden_ref, dgate_ref, dup_ref,
         x_ref, left_ref, right_ref, taps_ref, gain_ref, routes_ref, gates_ref,
         cot_ref, cots_ref, mixed_ref, scale_ref,
         out_ref, gin_ref, tap_ref, gain_out_ref, gg_ref, gwg_ref, gwu_ref, gwd_ref,
         by, bdx, sy, sdx, zdx, zy, rdx, ry, dots, norm, dm, dl, dr, tp,
         ds_, dr_, ys, yr, as_, ar, bs, br, gs, gr, qs, qr, hs, ts, tr):
    me, mine = lax.axis_index("ctx"), lax.axis_index("exp")
    chans, tokens = x_ref.shape
    slots, width = y_ref.shape
    taps = taps_ref.shape[0]
    half = taps // 2
    greet(n, m)
    own = pl.ds(pl.multiple_of(me * capacity, capacity), capacity)
    send_dx = parts(n, m, capacity, sdx, bdx, ds_, dr_)
    send_y = parts(n, m, capacity, sy, by, ys, yr)
    for k in range(m):
        sdx[k] = dx_ref[:, k * chans : (k + 1) * chans]
        send_dx[k].start()
        bdx[k, own] = sdx[k, own]
    for k in range(m):
        sy[k] = y_ref[:, k * chans : (k + 1) * chans]
        send_y[k].start()
        by[k, own] = sy[k, own]
    t0, t1 = picks(routes_ref[...], capacity, slots)
    p0, p1 = jnp.transpose(t0), jnp.transpose(t1)
    both = (p0 + p1).astype(BF16)
    gates = jnp.transpose(jnp.concatenate([gates_ref[...], jnp.zeros((6, tokens), F32)], axis=0))
    g0, g1 = gates[:, :1], gates[:, 1:2]
    p0, p1 = p0.astype(BF16), p1.astype(BF16)
    pack = columns(taps_ref, gain_ref, pad)
    grad_into(gwd_ref, hidden_ref, rdy_ref, min(256, hidden_ref.shape[1]))
    sum_dx = Exchange("exp", m, lambda p: zdx.at[p], lambda s: rdx.at[s], as_, ar)
    sum_y = Exchange("exp", m, lambda p: zy.at[p], lambda s: ry.at[s], bs, br)

    def when_other(k, exchange):
        @pl.when(mine != k)
        def _():
            exchange.to(lax.rem(k - mine + m, m)).start()

    for k in range(m):
        send_dx[k].arrive()
        zdx[k] = jnp.dot(both, bdx[k], preferred_element_type=F32).astype(BF16)
        when_other(k, sum_dx)
    rdx[mine] = zdx[mine]
    grad_into(gwg_ref, rx_ref, dgate_ref, min(256, width))
    x = x_ref[...].astype(F32)
    left, right = left_ref[...].astype(F32), right_ref[...].astype(F32)
    mixed = mixed_ref[...].astype(F32)
    gain = pack[:, taps : taps + 1]
    scale = scale_ref[:1]
    cot = cot_ref[...].astype(F32)
    sum_dx.arrive()
    dn = jnp.transpose(jnp.sum(rdx[...].astype(F32), axis=0))
    weighted = dn * mixed
    norm[mine] = jnp.broadcast_to(jnp.sum(weighted * gain, axis=0, keepdims=True), (8, tokens))
    sum_norm = Exchange("exp", m, lambda p: norm.at[mine], lambda s: norm.at[s], qs, qr)
    sum_norm.start()
    d0 = jnp.zeros((tokens, 1), F32)
    d1 = jnp.zeros((tokens, 1), F32)
    for k in range(m):
        send_y[k].arrive()
        y0 = jnp.dot(p0, by[k], preferred_element_type=F32)
        y1 = jnp.dot(p1, by[k], preferred_element_type=F32)
        zy[k] = (y0 * g0 + y1 * g1).astype(BF16)
        when_other(k, sum_y)
        turned = jnp.transpose(cots_ref[k].astype(F32))
        d0 = d0 + jnp.sum(y0 * turned, axis=1, keepdims=True)
        d1 = d1 + jnp.sum(y1 * turned, axis=1, keepdims=True)
    ry[mine] = zy[mine]
    col = lax.broadcasted_iota(jnp.int32, (tokens, 128), 1)
    dots[mine] = jnp.transpose(jnp.where(col == 0, d0, jnp.where(col == 1, d1, 0.0)))[:8]
    sum_dots = Exchange("exp", m, lambda p: dots.at[mine], lambda s: dots.at[s], gs, gr)
    sum_dots.start()
    lane = lax.broadcasted_iota(jnp.int32, (chans, tokens), 1)
    gain_grad = jnp.sum(weighted * scale, axis=1, keepdims=True)
    sum_norm.arrive()
    q = jnp.sum(norm[...], axis=0)[:1]
    d_mixed = cot + gain * dn * scale - mixed * (q * scale * scale * scale / width)
    dm[...] = d_mixed.astype(BF16)
    halo = Halo(n, dm, dl, dr, hs)
    halo.start()
    grads = jnp.where(lane == taps, gain_grad, 0.0)
    for j in range(taps):
        term = jnp.sum(d_mixed * shifted(x, left, right, j - half, lane), axis=1, keepdims=True)
        grads = jnp.where(lane == j, term, grads)
    tp[me] = jnp.transpose(grads)[:pad]
    sum_taps = Exchange("ctx", n, lambda p: tp.at[me], lambda s: tp.at[s], ts, tr)
    sum_taps.start()
    halo.arrive()
    dleft, dright = dl[...].astype(F32), dr[...].astype(F32)
    grad = d_mixed
    for j in range(taps):
        grad = grad + pack[:, j : j + 1] * shifted(d_mixed, dleft, dright, half - j, lane)
    gin_ref[...] = grad.astype(BF16)
    grad_into(gwu_ref, rx_ref, dup_ref, min(256, width))
    sum_y.arrive()
    out_ref[...] = (mixed + jnp.transpose(jnp.sum(ry[...].astype(F32), axis=0))).astype(BF16)
    sum_dots.arrive()
    gg_ref[...] = jnp.sum(dots[...], axis=0)[:2]
    sum_taps.arrive()
    total = jnp.sum(tp[...], axis=0)
    tap_ref[...] = total[:taps]
    gain_out_ref[...] = total[taps : taps + 1]
    for done in (*send_dx, *send_y, sum_dx, sum_y, sum_dots, sum_norm, halo, sum_taps):
        done.sent()


def hand_on(count, *refs):
    done = refs[2 * count]
    copies = [pltpu.make_async_copy(refs[i], refs[count + i], done.at[i]) for i in range(count)]
    for copy in copies:
        copy.start()
    for copy in copies:
        copy.wait()


def sems(*counts):
    out = []
    for count in counts:
        shape = count if isinstance(count, tuple) else (count,)
        out += [pltpu.SemaphoreType.DMA(shape), pltpu.SemaphoreType.DMA(shape)]
    return out


def local(inputs, conv_taps, norm_gain, routes, gate_probs, w_gate, w_up, w_down, grad_out):
    chans, tokens = inputs.shape
    taps = conv_taps.shape[1]
    width = w_gate.shape[1]
    n, m = lax.axis_size("ctx"), lax.axis_size("exp")
    capacity = max(tokens // 8, (2 * tokens + n - 1) // n)
    slots = n * capacity
    pad = -(-(taps + 1) // 8) * 8
    taps_t, gain_row = conv_taps.T, norm_gain.reshape(1, chans)
    routes_t, gates_t = routes.T, gate_probs.T
    vmem = pl.BlockSpec(memory_space=pltpu.VMEM)
    shape = jax.ShapeDtypeStruct
    rx, rdy, mixed, scale, left, right, cots = pl.pallas_call(
        functools.partial(front, n, m, capacity, pad),
        out_shape=(
            shape((slots, width), BF16),
            shape((slots, width), BF16),
            shape((chans, tokens), BF16),
            shape((8, tokens), F32),
            shape((chans, tokens), BF16),
            shape((chans, tokens), BF16),
            shape((m, chans, tokens), BF16),
        ),
        in_specs=[vmem] * 6,
        out_specs=(vmem,) * 7,
        scratch_shapes=[
            pltpu.VMEM((m, chans, tokens), BF16),
            pltpu.VMEM((m, 8, tokens), F32),
            *[pltpu.VMEM((m, slots, chans), BF16)] * 4,
            pltpu.SemaphoreType.DMA((4,)),
            *sems(m, m, m, (m, n), (m, n)),
        ],
        compiler_params=pltpu.CompilerParams(
            collective_id=0, has_side_effects=True, vmem_limit_bytes=40 << 20
        ),
        name="front",
    )(inputs, taps_t, gain_row, routes_t, gates_t, grad_out)
    weight_gate, weight_up, weight_down = w_gate[0], w_up[0], w_down[0]
    gate_act = jnp.dot(rx, weight_gate, preferred_element_type=F32)
    up_act = jnp.dot(rx, weight_up, preferred_element_type=F32)
    sigma = jax.nn.sigmoid(gate_act)
    hidden = (gate_act * sigma * up_act).astype(BF16)
    result = jnp.dot(hidden, weight_down, preferred_element_type=F32).astype(BF16)
    d_hidden = lax.dot_general(rdy, weight_down, LAST, preferred_element_type=F32)
    d_gate = (d_hidden * up_act * sigma * (1.0 + gate_act * (1.0 - sigma))).astype(BF16)
    d_up = (d_hidden * gate_act * sigma).astype(BF16)
    d_rows = lax.dot_general(d_gate, weight_gate, LAST, preferred_element_type=F32)
    d_rows = d_rows + lax.dot_general(d_up, weight_up, LAST, preferred_element_type=F32)
    d_rows = d_rows.astype(BF16)
    made = pl.pallas_call(
        functools.partial(back, n, m, capacity, pad),
        out_shape=(
            shape((chans, tokens), BF16),
            shape((chans, tokens), BF16),
            shape((taps, chans), F32),
            shape((1, chans), F32),
            shape((2, tokens), F32),
            shape(w_gate.shape[1:], BF16),
            shape(w_up.shape[1:], BF16),
            shape(w_down.shape[1:], BF16),
        ),
        in_specs=[vmem] * 18,
        out_specs=(vmem,) * 8,
        scratch_shapes=[
            *[pltpu.VMEM((m, slots, chans), BF16)] * 4,
            pltpu.VMEM((m, tokens, chans), BF16),
            pltpu.VMEM((m, tokens, chans), BF16),
            pltpu.VMEM((m, tokens, chans), BF16),
            pltpu.VMEM((m, tokens, chans), BF16),
            pltpu.VMEM((m, 8, tokens), F32),
            pltpu.VMEM((m, 8, tokens), F32),
            pltpu.VMEM((chans, tokens), BF16),
            pltpu.VMEM((chans, tokens), BF16),
            pltpu.VMEM((chans, tokens), BF16),
            pltpu.VMEM((n, pad, chans), F32),
            *sems((m, n), (m, n), m, m, m, m),
            pltpu.SemaphoreType.DMA((4,)),
            *sems(n),
        ],
        compiler_params=pltpu.CompilerParams(
            collective_id=1, has_side_effects=True, vmem_limit_bytes=40 << 20
        ),
        name="back",
    )(
        result, d_rows, rx, rdy, hidden, d_gate, d_up, inputs, left, right, taps_t, gain_row,
        routes_t, gates_t, grad_out, cots, mixed, scale,
    )
    anywhere = pl.BlockSpec(memory_space=pl.ANY)
    count = len(made)
    layer_out, grad_in, grad_taps, grad_gain, grad_gates, grad_gate, grad_up, grad_down = pl.pallas_call(
        functools.partial(hand_on, count),
        out_shape=tuple(shape(a.shape, a.dtype) for a in made),
        in_specs=[anywhere] * count,
        out_specs=(anywhere,) * count,
        scratch_shapes=[pltpu.SemaphoreType.DMA((count,))],
        name="hand_on",
    )(*made)
    return (
        layer_out,
        grad_in,
        grad_taps.T,
        grad_gain[0],
        grad_gates.T,
        grad_gate[None],
        grad_up[None],
        grad_down[None],
    )


def solution(mesh):
    return jax.shard_map(
        local,
        mesh=mesh,
        in_specs=(
            P("exp", "ctx"),
            P("exp", None),
            P("exp"),
            P("ctx", None),
            P("ctx", None),
            P("ctx", None, "exp"),
            P("ctx", None, "exp"),
            P("ctx", "exp", None),
            P("exp", "ctx"),
        ),
        out_specs=(
            P("exp", "ctx"),
            P("exp", "ctx"),
            P("exp", None),
            P("exp"),
            P("ctx", None),
            P("ctx", None, "exp"),
            P("ctx", None, "exp"),
            P("ctx", "exp", None),
        ),
        check_vma=False,
    )
```

time: 85.2 us -> 283 us (3.32)
  Pallas kernels: 63.1 us -> 263 us
  local copies, waits for them, and re-layouts: 5.29 us -> 12 us
  matrix products: 12.8 us -> 6.39 us
  other arithmetic: 2.94 us -> 0 us
    pallas_call x2 -> x3, Pallas kernels: 63.1 us -> 263 us  [the longest x1 197 us: local(): pl.pallas_call(functools.partial(hand_on, count), out_shape=tuple((shape(...]
    unnamed x12 -> x32, local copies, waits for them, and re-layouts: 3.34 us -> 11.2 us
    dot_general x3 -> x0, matrix products: 6.21 us -> none  [the longest x1 2.07 us: local(): lax.dot_general(hidden, rdy, FIRST, preferred_element_type=F32).astype(BF16)]
where the time goes in v2:
time: 283 us; the launch traced here: 282 us
  Pallas kernels  263 us (93%)
  local copies, waits for them, and re-layouts  12 us (4%)
  matrix products  6.39 us (2%)
    pallas_call x1, Pallas kernels, local(): pl.pallas_call(functools.partial(hand_on, count), out_shape=tuple((shape(...  197 us
    pallas_call x1, Pallas kernels, local(): pl.pallas_call(functools.partial(back, n, m, capacity, pad), out_shape=(s...  39.5 us
    pallas_call x1, Pallas kernels, local(): pl.pallas_call(functools.partial(front, n, m, capacity, pad), out_shape=(...  26.9 us
    unnamed x32, local copies, waits for them, and re-layouts  11.2 us

profile of v2, /device:TPU:1, one launch (start us, length us, event | category | flops | bytes accessed | tf_op | source)
XLA Modules:
  0.0 282.4 jit_solution(17237467817014318889)
XLA Ops:
  0.6 0.0 copy-start
  0.6 0.8 reshape.19.gain_ref
  1.5 0.0 copy-start.4
  1.5 0.8 copy-done.4
  2.3 0.0 copy-start.5
  2.3 0.8 copy-done.5
  3.1 0.0 copy-start.6
  3.1 0.8 copy-done.6
  3.9 0.7 copy-done.10
  4.6 0.7 copy-done.11
  5.3 26.9 %front.1 = (bf16[256,1024]{1,0:T(8,128)(2,1)S(1)}, bf16[256,1024]{1,0:T(8,128)(2,1)S(1)}, bf16[256,128]{1,0:T(8,128)(2,1)S(1)}, f32[8,128]{1,0:T(8,128)S(1)}, bf...) custom-call(bf16[256,128]{1,0:T(8,128)(2,1)S(1)} %copy-done.4, ...), custom_call_target="tpu_custom_call" | custom-call | tf_op jit(solution)/shard_map/front/pallas_call | solution.py:376
  32.1 2.3 fusion
  34.5 0.0 copy-done.14
  34.5 0.7 fusion.6
  35.2 0.0 copy-done
  35.2 0.0 copy-start.15
  35.2 1.2 multiply_convert_fusion.1
  36.4 0.4 copy-done.15
  36.8 0.7 fusion.15.y_ref
  37.5 0.7 fusion.4
  38.2 0.7 fusion.18.dx_ref
  39.0 39.5 %back.1 = (bf16[256,128]{1,0:T(8,128)(2,1)S(1)}, bf16[256,128]{1,0:T(8,128)(2,1)S(1)}, f32[31,256]{1,0:T(8,128)S(1)}, f32[1,256]{1,0:T(1,128)S(1)}, f32[2,128]{1...) custom-call(bf16[256,1024]{1,0:T(8,128)(2,1)S(1)} %fusion.15.y_ref, ...), custom_call_target="tpu_custom_call" | custom-call | tf_op jit(solution)/shard_map/back/pallas_call | solution.py:413
  78.5 0.0 copy-start.1
  78.5 1.3 copy-done.1
  79.8 1.3 copy-done.2
  81.2 1.4 copy-done.3
  82.5 0.6 copy-done.7
  83.1 0.6 copy-done.8
  83.8 0.6 copy-done.9
  84.4 0.5 copy-done.12
  84.9 0.6 copy-done.13
  85.5 196.8 %hand_on.1 = (bf16[256,128]{1,0:T(8,128)(2,1)}, bf16[256,128]{1,0:T(8,128)(2,1)}, f32[31,256]{1,0:T(8,128)}, f32[1,256]{1,0:T(1,128)}, f32[2,128]{1,0:T(2,128)},...) custom-call(bf16[256,128]{1,0:T(8,128)(2,1)} %copy-done.7, ...), custom_call_target="tpu_custom_call" | custom-call | tf_op jit(solution)/shard_map/hand_on/pallas_call | solution.py:453
  (10 shorter events, 0.0 us)
Async XLA Ops:
  0.6 34.5 %copy-start = (bf16[1,1024,1024]{2,1,0:T(8,128)(2,1)S(1)}, bf16[1,1024,1024]{2,1,0:T(8,128)(2,1)}, u32[]{:S(2)}) copy-start(bf16[1,1024,1024]{2,1,0:T(8,128)(2,1)} %param.14) | copy-start | bytes 6291460
  1.5 0.8 copy-start.4
  2.3 0.8 copy-start.5
  3.1 0.8 copy-start.6
  3.9 0.7 copy-start.10
  4.6 0.7 copy-start.11
  5.3 29.2 %copy-start.14 = (bf16[1,1024,1024]{2,1,0:T(8,128)(2,1)S(1)}, bf16[1,1024,1024]{2,1,0:T(8,128)(2,1)}, u32[]{:S(2)}) copy-start(bf16[1,1024,1024]{2,1,0:T(8,128)(2,1)} %param.15) | copy-start | bytes 6291460
  35.2 1.6 copy-start.15
  78.5 1.3 copy-start.1
  79.8 1.3 copy-start.2
  81.2 1.4 copy-start.3
  82.5 0.6 copy-start.7
  83.1 0.6 copy-start.8
  83.8 0.6 copy-start.9
  84.4 0.5 copy-start.12
  84.9 0.6 copy-start.13
